TPU v7x, 32 devices: a whole 2x2x4 slice. The times are simulated.
32 devices in a mesh: scen: 4 (over x, core), own: 8 (over z, y).
Axes of the slice: x: 2, y: 2, z: 4, core: 2. Of those that a mesh axis runs over, the one named last changes fastest.
Arguments:
- kinv: bfloat16 [128, 1024, 1024], P(('scen', 'own'))
- coupling: bfloat16 [128, 1024, 768], P(('scen', 'own')), may hold values from -0.09375 to 0.09375
- residual: float32 [128, 1024], P(('scen', 'own')), may hold values from -6 to 6
- first_step: float32 [16384], P('own'), may hold values from -6 to 6
- links: int32 [128, 6], P(('scen', 'own')), may hold values from 0 to 127, as said below
- counts: int32 [128], P(('scen', 'own')), may hold values from 2 to 6
- owner_map: int32 [128], replicated, may hold values from 0 to 7, as said below
Outputs:
- schur_band: float32 [8, 2048, 1920], P('own', 'scen')
- second_step: float32 [128, 1024], P(('scen', 'own'))
Inputs may be any that keep to these rules, and one draw needn't show every extreme that they name: `owner_map`: every 8 consecutive linking blocks have distinct owners, and each owner has 16 blocks. `links`: the 6 slots of a scenario name distinct blocks. The 4 scenarios of one device couple only to blocks of one run of 8 consecutive linking blocks, and all of them name one common block in slot 0.
All inputs are finite; a program needn't handle non-finite values.
Results may differ from a plain program's by a relative error of at most 0.003.
Values may be sent and summed in bfloat16 or wider, within the bound.
A program may use at most 192 MiB of HBM per device.

v0:
```python
import jax
import jax.numpy as jnp
from jax import lax
from jax.sharding import PartitionSpec as P

BS = 128
NB = 128
K = 6
W = 8
R = 1024


def lookup(lookup_table, index_array):
    matches = index_array[..., None] == jnp.arange(lookup_table.shape[0], dtype=jnp.int32)
    return jnp.sum(jnp.where(matches, lookup_table, 0), axis=-1)


def place_blocks(blocks, row_ids, col_ids, live_flags, owner_rank, row_blocks):
    band_width = 2 * W - 1
    segment_ids = lookup(owner_rank, row_ids) * band_width + col_ids - row_ids + (W - 1)
    segment_ids = jnp.where(live_flags > 0, segment_ids, 0)
    summed = jax.ops.segment_sum(blocks, segment_ids, num_segments=row_blocks * band_width)
    arranged = summed.reshape(row_blocks, band_width, BS, BS).transpose(0, 2, 1, 3)
    return arranged.reshape(row_blocks * BS, band_width * BS)


def local(kinv, coupling, residual, first_step, links, counts, owner_map):
    scen_count = kinv.shape[0]
    owner_count = lax.axis_size("own")
    row_blocks = NB // owner_count
    highest = lax.Precision.HIGHEST
    live_slots = jnp.arange(K, dtype=jnp.int32)[None, :] < counts[:, None]
    coupled = jnp.where(live_slots[:, None, :, None], coupling.reshape(scen_count, R, K, BS), 0)
    coupled = coupled.reshape(scen_count, R, K * BS)
    solved = jnp.einsum("srt,stc->src", kinv, coupled, preferred_element_type=jnp.float32).astype(
        jnp.bfloat16
    )
    contrib = jnp.einsum("srk,src->skc", coupled, solved, preferred_element_type=jnp.float32)
    strips = contrib.reshape(scen_count, K, BS, K * BS)
    positions = jnp.arange(NB, dtype=jnp.int32)
    same_owner = owner_map[:, None] == owner_map[None, :]
    earlier = positions[None, :] < positions[:, None]
    owner_rank = jnp.sum(same_owner & earlier, axis=1)
    owner_ids = jnp.arange(owner_count, dtype=jnp.int32)
    owner_of = lookup(owner_map, links)
    picked_owner = (owner_of[..., None] == owner_ids).astype(jnp.int32)
    outgoing = jnp.einsum(
        "sko,skpc->ospc", picked_owner.astype(jnp.float32), strips, precision=highest
    )
    out_rows = jnp.sum(picked_owner * links[:, :, None], axis=1).T
    out_live = jnp.sum(picked_owner, axis=1).T
    out_cols = jnp.broadcast_to(links[None], (owner_count, scen_count, K))
    incoming, in_rows, in_live, in_cols = (
        lax.all_to_all(outgoing, "own", split_axis=0, concat_axis=0, tiled=True),
        lax.all_to_all(out_rows, "own", split_axis=0, concat_axis=0, tiled=True),
        lax.all_to_all(out_live, "own", split_axis=0, concat_axis=0, tiled=True),
        lax.all_to_all(out_cols, "own", split_axis=0, concat_axis=0, tiled=True),
    )
    blocks = (
        incoming.reshape(owner_count, scen_count, BS, K, BS)
        .transpose(0, 1, 3, 2, 4)
        .reshape(-1, BS, BS)
    )
    row_ids = jnp.broadcast_to(in_rows[:, :, None], (owner_count, scen_count, K)).reshape(-1)
    live_flags = jnp.broadcast_to(in_live[:, :, None], (owner_count, scen_count, K)).reshape(-1)
    col_ids = in_cols.reshape(-1)
    band_sum = place_blocks(blocks, row_ids, col_ids, live_flags, owner_rank, row_blocks)
    full_step = lax.all_gather(first_step.astype(jnp.bfloat16), "own", axis=0, tiled=True)
    step_table = full_step.reshape(NB, BS)
    picked = step_table[links].reshape(scen_count, K * BS)
    product = jnp.einsum("src,sc->sr", coupled, picked, preferred_element_type=jnp.float32)
    reduced_rhs = (residual - product).astype(jnp.bfloat16)
    second_step = jnp.einsum("srt,st->sr", kinv, reduced_rhs, preferred_element_type=jnp.float32)
    owned_rows = lax.psum_scatter(band_sum, "scen", scatter_dimension=0, tiled=True)
    return (owned_rows[None], second_step)


def solution(mesh):
    placed = (
        P(("scen", "own"), None, None),
        P(("scen", "own"), None, None),
        P(("scen", "own"), None),
        P("own"),
        P(("scen", "own"), None),
        P(("scen", "own")),
        P(),
    )
    return jax.shard_map(
        local,
        mesh=mesh,
        in_specs=placed,
        out_specs=(P("own", "scen", None), P(("scen", "own"), None)),
        check_vma=False,
    )
```

profile of v0, /device:TPU:11, one launch (start us, length us, event | category | flops | bytes accessed | tf_op | source)
XLA Modules:
  0.0 600.4 jit_solution(6905103868559931232)
XLA Ops:
  7.2 0.8 copy.62
  7.9 0.9 select_reduce_fusion.2
  8.8 0.1 copy.63
  8.9 0.9 select_reduce_fusion.1
  9.8 0.7 copy.67
  10.5 5.7 all-to-all-start.1
  16.2 0.7 iota_compare_fusion.5
  17.0 0.1 broadcast_bitcast_fusion
  17.0 0.7 copy.64
  17.7 2.6 all-to-all-done.1
  20.3 4.4 all-to-all-start
  24.7 0.0 copy-start
  24.7 18.5 %fusion.2 = f32[4,768,768]{2,1,0:T(8,128)} fusion(bf16[4,1024,768]{2,1,0:T(8,128)(2,1)} %param.8, pred[4,768]{1,0:T(4,128)(4,1)S(1)} %bitcast.68, bf16[4,1024,1024]{2,1,0:T(8,128)(2,1)} %param.7), kind=kOutput, calls=%fused_computation.5 | convolution fusion | flops 11283726336 | bytes 24120320 | tf_op jit(solution)/shard_map/srk,src->skc/dot_general | solution.py:38
  43.2 0.0 all-to-all-done
  43.2 0.0 copy-done
  43.2 0.6 broadcast_in_dim.85
  43.8 5.5 all-to-all-start.2
  49.3 22.7 %fusion.6 = f32[8,4,128,768]{3,0,2,1:T(8,128)} fusion(f32[4,6,128,768]{3,2,1,0:T(8,128)} %bitcast.59, s32[4,6]{1,0:T(4,128)S(1)} %copy.63), kind=kOutput, calls=%fused_computation.10 | convolution fusion | flops 226492992 | bytes 22020192 | tf_op jit(solution)/shard_map/sko,skpc->ospc/dot_general | solution.py:47
  71.9 13.1 %copy.73 = f32[8,4,128,768]{3,2,1,0:T(8,128)} copy(f32[8,4,128,768]{3,0,2,1:T(8,128)} %fusion.6) | data formatting | bytes 25165824 | tf_op jit(solution)/shard_map/sko,skpc->ospc/transpose | solution.py:47
  85.0 0.0 copy-start.3
  85.0 0.0 all-to-all-done.2
  85.0 5.6 all-to-all-start.3
  90.6 0.0 reduce-scatter.2.cloned.1.call-start
  90.6 0.0 copy-done.3
  90.6 0.2 convert_reduce_fusion
  90.8 0.1 broadcast_in_dim.82
  90.8 0.1 eq.60
  91.0 0.1 reshape.119
  91.1 0.1 copy.65
  91.2 0.1 copy.66
  91.3 0.1 broadcast_in_dim.80
  91.3 0.1 gt.25
  91.5 0.2 select_reduce_fusion
  91.7 0.1 reshape.118
  91.8 270.0 %all-to-all-done.3 = f32[8,4,128,768]{3,2,1,0:T(8,128)} async-done(((f32[8,4,128,768]{3,2,1,0:T(8,128)}), f32[8,4,128,768]{3,2,1,0:T(8,128)}, u32[]{:S(2)}, u32[]{:S(2)}) %all-to-all-start.3) | async-done | bytes 12582944 | tf_op jit(solution)/shard_map/all_to_all | solution.py:54
  361.8 12.6 %copy.74 = f32[8,4,128,768]{2,3,1,0:T(8,128)} copy(f32[8,4,128,768]{3,2,1,0:T(8,128)} %all-to-all-done.3) | data formatting | bytes 25165824 | tf_op jit(solution)/shard_map/all_to_all | solution.py:54
  374.4 12.7 %copy.75 = f32[8,4,6,128,128]{4,3,2,1,0:T(8,128)} copy(f32[8,4,6,128,128]{3,4,2,1,0:T(8,128)} %bitcast.57) | data formatting | bytes 25165824 | tf_op jit(solution)/shard_map/transpose | solution.py:61
  387.1 7.5 %broadcast_in_dim.77 = f32[240,128,128]{2,1,0:T(8,128)} broadcast(f32[]{:T(128)} %constant.6.clone.1), dimensions={} | broadcast | bytes 15728644 | tf_op jit(solution)/shard_map/broadcast_in_dim | solution.py:22
  394.6 39.0 %scatter_fusion = f32[240,128,128]{2,1,0:T(8,128)} fusion(f32[240,128,128]{2,1,0:T(8,128)} %broadcast_in_dim.77, s32[192]{0:T(256)S(1)} %bitcast.66, f32[192,128,128]{2,1,0:T(8,128)} %bitcast.58), kind=kCustom, calls=%fused_computation.1 | custom fusion | flops 3145728 | bytes 37749504 | tf_op jit(solution)/shard_map/scatter-add | solution.py:22
  433.6 15.8 %copy.76 = f32[16,128,15,128]{1,0,3,2:T(8,128)} copy(f32[16,128,15,128]{3,1,2,0:T(8,128)} %bitcast.54) | data formatting | bytes 31457280 | tf_op jit(solution)/shard_map/transpose | solution.py:23
  449.3 18.9 %copy.100 = f32[240,8,16,128]{3,1,2,0:T(8,128)} copy(f32[240,8,16,128]{3,2,1,0:T(8,128)} %bitcast.56) | data formatting | bytes 31457280
  468.2 0.0 copy-start.2
  468.2 0.0 reduce-scatter.2.cloned.1.call-update
  468.2 0.7 copy-done.2
  468.9 0.0 copy-start.1
  468.9 0.1 reshape.129
  469.0 22.9 %all_gather.3 = bf16[16384]{0:T(1024)(128)(2,1)S(1)} all-gather(bf16[2048]{0:T(1024)(128)(2,1)S(1)} %convert_element_type.25), channel_id=1, replica_groups=mesh['scen'=4,'own'=8] {'own'}, dimensions={0}, use_global_device_ids=true | all-gather | bytes 36864 | tf_op jit(solution)/shard_map/all_gather | solution.py:68
  491.8 0.6 gather_fusion
  492.4 4.8 fusion.4
  497.3 0.0 copy-done.1
  497.3 5.6 fusion.16
  503.0 0.6 copy.101
  503.6 84.6 %reduce-scatter.2.cloned.1.call-done = f32[512,1920]{0,1:T(8,128)} async-done(((f32[2048,1920]{0,1:T(8,128)}), f32[512,1920]{0,1:T(8,128)}) %reduce-scatter.2.cloned.1.call-update) | async-done | bytes 3932176 | tf_op jit(solution)/shard_map/reduce_scatter | solution.py:74
  588.1 5.4 copy.77
  (9 shorter events, 0.1 us)
Async XLA Ops:
  10.5 9.8 %all-to-all-start.1 = ((s32[8,1,4]{2,1,0:T(1,128)}), s32[8,1,4]{2,1,0:T(1,128)S(1)}, u32[]{:S(2)}, u32[]{:S(2)}) async-start(s32[8,1,4]{2,1,0:T(1,128)} %copy.67), calls=%async_computation.1 | async-start | bytes 8192 | tf_op jit(solution)/shard_map/all_to_all | solution.py:55
  20.3 22.9 %all-to-all-start = ((s32[8,1,4]{2,1,0:T(1,128)}), s32[8,1,4]{2,1,0:T(1,128)S(1)}, u32[]{:S(2)}, u32[]{:S(2)}) async-start(s32[8,1,4]{2,1,0:T(1,128)} %copy.64), calls=%async_computation | async-start | bytes 8192 | tf_op jit(solution)/shard_map/all_to_all | solution.py:56
  24.7 18.5 %copy-start = (s32[4,6]{1,0:T(4,128)S(1)}, s32[4,6]{1,0:T(4,128)}, u32[]{:S(2)}) copy-start(s32[4,6]{1,0:T(4,128)} %param.11) | copy-start | bytes 292
  43.8 41.2 %all-to-all-start.2 = ((s32[8,4,6]{2,1,0:T(4,128)}), s32[8,4,6]{2,1,0:T(4,128)S(1)}, u32[]{:S(2)}, u32[]{:S(2)}) async-start(s32[8,4,6]{2,1,0:T(4,128)} %broadcast_in_dim.85), calls=%async_computation.2 | async-start | bytes 32768 | tf_op jit(solution)/shard_map/all_to_all | solution.py:57
  85.0 5.6 copy-start.3
  85.0 276.8 %all-to-all-start.3 = ((f32[8,4,128,768]{3,2,1,0:T(8,128)}), f32[8,4,128,768]{3,2,1,0:T(8,128)}, u32[]{:S(2)}, u32[]{:S(2)}) async-start(f32[8,4,128,768]{3,2,1,0:T(8,128)} %copy.73), calls=%async_computation.3 | async-start | bytes 25165824 | tf_op jit(solution)/shard_map/all_to_all | solution.py:54
  90.6 497.6 %reduce-scatter.2.cloned.1.call-start = ((), (), s32[]{:S(2)}) async-start(), calls=%async_computation.5 | async-start | bytes 19660800 | tf_op jit(solution)/shard_map/reduce_scatter | solution.py:74
  468.2 0.7 copy-start.2
  468.9 28.4 %copy-start.1 = (f32[4,1024]{1,0:T(4,128)S(1)}, f32[4,1024]{1,0:T(4,128)}, u32[]{:S(2)}) copy-start(f32[4,1024]{1,0:T(4,128)} %param.9) | copy-start | bytes 49156
Sparse Core Ops, SparseCore 0:
  468.3 119.7 reduce-scatter.1
where the time goes:
time: 605 us; the launch traced here: 600 us
  waiting for transfers between devices  357 us (59%)
  local copies, waits for them, and re-layouts  91.6 us (15%)
  matrix products  51.6 us (9%)
  other arithmetic  41.9 us (7%)
  blocking collectives  22.9 us (4%)
  starting transfers between devices  21.2 us (4%)
  between operations  14.1 us (2%)
    all_to_all x1, waiting for transfers between devices, local(): lax.all_to_all(outgoing, 'own', split_axis=0, concat_axis=0, tiled=True)  270 us
    reduce_scatter x1, waiting for transfers between devices, local(): lax.psum_scatter(band_sum, 'scen', scatter_dimension=0, tiled=True)  84.6 us
    scatter-add x1, other arithmetic, place_blocks(): jax.ops.segment_sum(blocks, segment_ids, num_segments=row_blocks * band_w...  39 us
    unnamed x13, local copies, waits for them, and re-layouts  25.8 us
    all_gather x1, blocking collectives, local(): lax.all_gather(first_step.astype(jnp.bfloat16), 'own', axis=0, tiled=True)  22.9 us
    dot_general x1, matrix products, local(): jnp.einsum('sko,skpc->ospc', picked_owner.astype(jnp.float32), strips, pr...  22.7 us
    dot_general x1, matrix products, local(): jnp.einsum('srk,src->skc', coupled, solved, preferred_element_type=jnp.fl...  18.5 us
    transpose x1, local copies, waits for them, and re-layouts, place_blocks(): summed.reshape(row_blocks, band_width, BS, BS).transpose(0, 2, 1, 3)  15.8 us
  transfers between devices with their start and end apart: 5, of which 3 were waited for; matrix products, arithmetic and copies ran while one was open for 11% of the time, Pallas kernels for 0%

commit v1 on v0

v1 whole, which is shorter than its diff:
```python
import functools

import jax
import jax.numpy as jnp
from jax import lax
from jax.experimental import pallas as pl
from jax.experimental.pallas import tpu as pltpu
from jax.sharding import PartitionSpec as P

BS = 128
NB = 128
K = 6
W = 8
R = 1024
BAND = (2 * W - 1) * BS
WIN = W * BS
MESH = pl.DeviceIdType.MESH
TN = (((0,), (0,)), ((), ()))
NT = (((1,), (1,)), ((), ()))


def window_kernel(rows_ref, cols_ref, counts_ref, kinv_ref, coup_ref, out_ref, win):
    s = pl.program_id(0)

    @pl.when(s == 0)
    def _():
        win[...] = jnp.zeros_like(win)

    count = counts_ref[s]
    slot = lax.broadcasted_iota(jnp.int32, (R, K * BS), 1) // BS
    coupled = jnp.where(slot < count, coup_ref[0], jnp.zeros((), jnp.bfloat16))
    solved = jnp.dot(kinv_ref[0], coupled, preferred_element_type=jnp.float32)
    solved = solved.astype(jnp.bfloat16)
    for i in range(K):

        @pl.when(i < count)
        def _():
            strip = lax.dot_general(
                coup_ref[0, :, i * BS : (i + 1) * BS],
                solved,
                TN,
                preferred_element_type=jnp.float32,
            )
            row = pl.multiple_of(rows_ref[s * K + i] * BS, BS)
            for j in range(K):
                col = pl.multiple_of(cols_ref[s * K + j] * BS, BS)
                win[pl.ds(row, BS), pl.ds(col, BS)] += strip[:, j * BS : (j + 1) * BS]

    @pl.when(s == pl.num_programs(0) - 1)
    def _():
        out_ref[...] = win[...].astype(jnp.bfloat16)


def windows(rows, cols, counts, kinv, coupling, owners):
    scen_count = kinv.shape[0]
    return pl.pallas_call(
        window_kernel,
        out_shape=jax.ShapeDtypeStruct((owners * BS, WIN), jnp.bfloat16),
        grid_spec=pltpu.PrefetchScalarGridSpec(
            num_scalar_prefetch=3,
            grid=(scen_count,),
            in_specs=[
                pl.BlockSpec((1, R, R), lambda s, *_: (s, 0, 0)),
                pl.BlockSpec((1, R, K * BS), lambda s, *_: (s, 0, 0)),
            ],
            out_specs=pl.BlockSpec((owners * BS, WIN), lambda s, *_: (0, 0)),
            scratch_shapes=[pltpu.VMEM((owners * BS, WIN), jnp.float32)],
        ),
        compiler_params=pltpu.CompilerParams(vmem_limit_bytes=56 * 2**20),
    )(rows, cols, counts, kinv, coupling)


def flip(index, bits, size):
    result = 0
    weight = 1
    while weight < size:
        bit = (index // weight) % 2
        if (bits // weight) % 2:
            bit = 1 - bit
        result = result + bit * weight
        weight *= 2
    return result


def exchange_kernel(
    groups, owners, rows_ref, meta_ref, all_rows, all_meta,
    own_send, own_recv, x_send, x_recv, core_send, core_recv,
    meta_send, meta_recv, meta2_send, meta2_recv, local_sem,
):
    g = lax.axis_index("scen")
    o = lax.axis_index("own")
    chips = groups // 2
    core = g % 2
    x = g // 2
    sibling = x * 2 + 1 - core
    xs = [flip(x, b, chips) * 2 + core for b in range(chips)]
    partner = [flip(o, k, owners) for k in range(owners)]

    barrier = pltpu.get_barrier_semaphore()
    for k in range(1, owners):
        pl.semaphore_signal(barrier, inc=1, device_id=(g, partner[k]), device_id_type=MESH)
    others = [flip(g, b, groups) for b in range(1, groups)]
    for other in others:
        pl.semaphore_signal(barrier, inc=1, device_id=(other, o), device_id_type=MESH)
    pl.semaphore_wait(barrier, owners - 1 + groups - 1)

    def remote(src, dst, send, recv, device):
        return pltpu.make_async_remote_copy(
            src_ref=src, dst_ref=dst, send_sem=send, recv_sem=recv,
            device_id=device, device_id_type=MESH,
        )

    own = [None] * owners
    for k in range(1, owners):
        own[k] = remote(
            rows_ref.at[partner[k]], all_rows.at[g, o], own_send.at[k], own_recv.at[k], (g, partner[k])
        )
    meta = [None] * owners
    for k in range(1, owners):
        meta[k] = remote(
            meta_ref, all_meta.at[g, o], meta_send.at[k], meta_recv.at[k], (g, partner[k])
        )
    keep_rows = pltpu.make_async_copy(rows_ref.at[o], all_rows.at[g, o], local_sem.at[0])
    keep_meta = pltpu.make_async_copy(meta_ref, all_meta.at[g, o], local_sem.at[1])

    far = list(range(owners // 2, owners))
    near = list(range(1, owners // 2))
    keep_meta.start()
    for k in range(1, owners):
        meta[k].start()
    own[far[0]].start()
    own[far[1]].start()
    keep_rows.start()
    for k in near:
        own[k].start()

    x_copies = {}
    core_copies = {}

    def forward(k):
        h = partner[k]
        src = rows_ref.at[o] if k == 0 else all_rows.at[g, h]
        for b in range(1, chips):
            x_copies[b, k] = remote(
                src, all_rows.at[g, h], x_send.at[b, k], x_recv.at[b, k], (xs[b], o)
            )
            x_copies[b, k].start()
        core_copies[0, k] = remote(
            src, all_rows.at[g, h], core_send.at[0, k], core_recv.at[0, k], (sibling, o)
        )
        core_copies[0, k].start()

    def forward_x(k):
        h = partner[k]
        for b in range(1, chips):
            x_copies[b, k].wait_recv()
            place = all_rows.at[xs[b], h]
            core_copies[b, k] = remote(
                place, place, core_send.at[b, k], core_recv.at[b, k], (sibling, o)
            )
            core_copies[b, k].start()

    forward(0)
    meta2 = []
    keep_meta.wait()
    for k in range(1, owners):
        meta[k].wait()
    for b, other in enumerate(others):
        copy = remote(
            all_meta.at[g], all_meta.at[g], meta2_send.at[b], meta2_recv.at[b], (other, o)
        )
        copy.start()
        meta2.append(copy)
    done = [0]
    for k in near:
        own[k].wait_recv()
        forward(k)
        done.append(k)
    behind = 0
    for n, k in enumerate(far):
        if n + 2 < len(far):
            own[k].wait_send()
            own[far[n + 2]].start()
        own[k].wait_recv()
        forward(k)
        done.append(k)
        while behind < len(done) - 2:
            forward_x(done[behind])
            behind += 1
    while behind < len(done):
        forward_x(done[behind])
        behind += 1
    for copy in meta2:
        copy.wait()
    keep_rows.wait()
    for k in near + far[-2:]:
        own[k].wait_send()
    for k in range(owners):
        for b in range(1, chips):
            x_copies[b, k].wait_send()
        for b in range(chips):
            core_copies[b, k].wait()


def exchange(rows, meta, groups, owners):
    any_space = pl.BlockSpec(memory_space=pl.ANY)
    dma = pltpu.SemaphoreType.DMA
    return pl.pallas_call(
        functools.partial(exchange_kernel, groups, owners),
        out_shape=(
            jax.ShapeDtypeStruct((groups, owners, BS, WIN), jnp.bfloat16),
            jax.ShapeDtypeStruct((groups, owners) + meta.shape, jnp.float32),
        ),
        in_specs=[any_space, any_space],
        out_specs=(any_space, any_space),
        scratch_shapes=[
            dma((owners,)), dma((owners,)),
            dma((groups // 2, owners)), dma((groups // 2, owners)),
            dma((groups // 2, owners)), dma((groups // 2, owners)),
            dma((owners,)), dma((owners,)),
            dma((groups,)), dma((groups,)),
            dma((2,)),
        ],
        compiler_params=pltpu.CompilerParams(collective_id=0, has_side_effects=True),
    )(rows, meta)


def place_kernel(
    blocks, sources, codes_ref, links_ref, counts_ref, base_ref,
    kinv_ref, coup_ref, residual_ref, table_ref, rows_ref, band_ref, step_ref, held, sems,
):
    s = pl.program_id(0)
    base = base_ref[0]

    def copy_of(n):
        return pltpu.make_async_copy(rows_ref.at[n], held.at[n], sems.at[n])

    @pl.when(s == 0)
    def _():
        def begin(n, carry):
            rank = codes_ref[n] // W - base

            @pl.when((codes_ref[n] >= 0) & (rank >= 0) & (rank < blocks))
            def _():
                copy_of(n).start()

            return carry

        lax.fori_loop(0, sources, begin, 0)

    count = counts_ref[s]
    parts = []
    for k in range(K):
        row = table_ref[pl.ds(links_ref[s * K + k], 1), :]
        parts.append(jnp.where(k < count, row, 0.0))
    picked = jnp.broadcast_to(jnp.concatenate(parts, axis=1), (16, K * BS)).astype(jnp.bfloat16)
    product = lax.dot_general(picked, coup_ref[0], NT, preferred_element_type=jnp.float32)
    reduced = (residual_ref[pl.ds(s, 1), :] - product).astype(jnp.bfloat16)
    step = lax.dot_general(reduced, kinv_ref[0], NT, preferred_element_type=jnp.float32)
    step_ref[pl.ds(s, 1), :] = step[:1]

    @pl.when(s < blocks)
    def _():
        band_ref[...] = jnp.zeros_like(band_ref)

        def add(n, carry):
            code = codes_ref[n]

            @pl.when((code >= 0) & (code // W - base == s))
            def _():
                copy_of(n).wait()
                col = pl.multiple_of((W - 1 - code % W) * BS, BS)
                band_ref[:, pl.ds(col, WIN)] += held[n].astype(jnp.float32)

            return carry

        lax.fori_loop(0, sources, add, 0)


def place(codes, links, counts, base, kinv, coupling, residual, table, rows, blocks):
    scen_count = kinv.shape[0]
    sources = rows.shape[0]
    assert blocks <= scen_count
    return pl.pallas_call(
        functools.partial(place_kernel, blocks, sources),
        out_shape=(
            jax.ShapeDtypeStruct((blocks * BS, BAND), jnp.float32),
            jax.ShapeDtypeStruct((scen_count, R), jnp.float32),
        ),
        grid_spec=pltpu.PrefetchScalarGridSpec(
            num_scalar_prefetch=4,
            grid=(scen_count,),
            in_specs=[
                pl.BlockSpec((1, R, R), lambda s, *_: (s, 0, 0)),
                pl.BlockSpec((1, R, K * BS), lambda s, *_: (s, 0, 0)),
                pl.BlockSpec((scen_count, R), lambda s, *_: (0, 0)),
                pl.BlockSpec((NB, BS), lambda s, *_: (0, 0)),
                pl.BlockSpec(memory_space=pl.ANY),
            ],
            out_specs=(
                pl.BlockSpec((BS, BAND), lambda s, *_: (jnp.minimum(s, blocks - 1), 0)),
                pl.BlockSpec((scen_count, R), lambda s, *_: (0, 0)),
            ),
            scratch_shapes=[
                pltpu.VMEM((sources, BS, WIN), jnp.bfloat16),
                pltpu.SemaphoreType.DMA((sources,)),
            ],
        ),
        compiler_params=pltpu.CompilerParams(vmem_limit_bytes=58 * 2**20),
    )(codes, links, counts, base, kinv, coupling, residual, table, rows)


def local(kinv, coupling, residual, first_step, links, counts, owner_map):
    groups = lax.axis_size("scen")
    owners = lax.axis_size("own")
    row_blocks = NB // owners
    blocks = row_blocks // groups
    positions = jnp.arange(NB, dtype=jnp.int32)
    same_owner = owner_map[:, None] == owner_map[None, :]
    rank = jnp.sum(same_owner & (positions[None, :] < positions[:, None]), axis=1, dtype=jnp.int32)
    start = jnp.min(links)
    inside = (positions >= start) & (positions < start + W)
    lanes = jnp.arange(BS, dtype=jnp.int32)
    holds = inside[:, None] & (owner_map[:, None] == lanes[None, :])
    codes = jnp.sum(jnp.where(holds, (rank * W + positions - start + 1)[:, None], 0), axis=0) - 1
    flat_links = links.reshape(-1)
    owner_of = jnp.sum(
        jnp.where(flat_links[:, None] == positions[None, :], owner_map[None, :], 0), axis=1
    )
    rows = windows(owner_of, flat_links - start, counts, kinv, coupling, owners)
    table_rows = first_step.shape[0] // BS
    meta = jnp.concatenate(
        [
            first_step.reshape(table_rows, BS),
            jnp.broadcast_to(codes.astype(jnp.float32)[None], (8, BS)),
        ],
        axis=0,
    )
    all_rows, all_meta = exchange(rows.reshape(owners, BS, WIN), meta, groups, owners)
    g = lax.axis_index("scen")
    o = lax.axis_index("own")
    table = all_meta[0, :, :table_rows].reshape(NB, BS)
    mine = jnp.sum(
        jnp.where(lanes == o, all_meta[:, :, table_rows].reshape(groups * owners, BS), 0.0), axis=1
    ).astype(jnp.int32)
    band, second_step = place(
        mine, flat_links, counts, (g * blocks).reshape(1), kinv, coupling, residual, table,
        all_rows.reshape(groups * owners, BS, WIN), blocks,
    )
    return band[None], second_step


def solution(mesh):
    placed = (
        P(("scen", "own"), None, None),
        P(("scen", "own"), None, None),
        P(("scen", "own"), None),
        P("own"),
        P(("scen", "own"), None),
        P(("scen", "own")),
        P(),
    )
    return jax.shard_map(
        local,
        mesh=mesh,
        in_specs=placed,
        out_specs=(P("own", "scen", None), P(("scen", "own"), None)),
        check_vma=False,
    )
```

time: 605 us -> 111 us (0.18)
  waiting for transfers between devices: 357 us -> 0 us
  Pallas kernels: 0 us -> 98 us
  local copies, waits for them, and re-layouts: 91.6 us -> 2.8 us
  matrix products: 51.6 us -> 0 us
  other arithmetic: 41.9 us -> 9.26 us
  blocking collectives: 22.9 us -> 0 us
  starting transfers between devices: 21.2 us -> 0 us
  between operations: 14.1 us -> 1.34 us
    all_to_all x4 -> x0, waiting for transfers between devices: 273 us -> none  [the longest x1 270 us: local(): lax.all_to_all(outgoing, 'own', split_axis=0, concat_axis=0, tiled=True)]
    pallas_call x0 -> x3, Pallas kernels: none -> 98 us  [the longest x1 68.5 us: exchange(): pl.pallas_call(functools.partial(exchange_kernel, groups, owners), out_sh...]
    reduce_scatter x1 -> x0, waiting for transfers between devices: 84.6 us -> none  [local(): lax.psum_scatter(band_sum, 'scen', scatter_dimension=0, tiled=True)]
    dot_general x4 -> x0, matrix products: 51.6 us -> none  [the longest x1 22.7 us: local(): jnp.einsum('sko,skpc->ospc', picked_owner.astype(jnp.float32), strips, pr...]
    transpose x3 -> x0, local copies, waits for them, and re-layouts: 41.5 us -> none  [the longest x1 15.8 us: place_blocks(): summed.reshape(row_blocks, band_width, BS, BS).transpose(0, 2, 1, 3)]
    scatter-add x1 -> x0, other arithmetic: 39 us -> none  [place_blocks(): jax.ops.segment_sum(blocks, segment_ids, num_segments=row_blocks * band_w...]
    unnamed x13 -> x2, local copies, waits for them, and re-layouts: 25.8 us -> 0.01 us
    all_gather x1 -> x0, blocking collectives: 22.9 us -> none  [local(): lax.all_gather(first_step.astype(jnp.bfloat16), 'own', axis=0, tiled=True)]
  transfers between devices with their start and end apart: 5 -> 0, of which waited for: 3 -> 0; matrix products, arithmetic and copies ran while one was open for 11% -> 0% of each run, Pallas kernels for 0% -> 0%
where the time goes in v1:
time: 111 us
  Pallas kernels  98 us (88%)
  other arithmetic  9.26 us (8%)
  local copies, waits for them, and re-layouts  2.8 us (3%)
  between operations  1.34 us (1%)
    pallas_call x1, Pallas kernels, exchange(): pl.pallas_call(functools.partial(exchange_kernel, groups, owners), out_sh...  68.5 us
    pallas_call x1, Pallas kernels, windows(): pl.pallas_call(window_kernel, out_shape=jax.ShapeDtypeStruct((owners * BS...  17.4 us
    pallas_call x1, Pallas kernels, place(): pl.pallas_call(functools.partial(place_kernel, blocks, sources), out_shap...  12.1 us

profile of v1, /device:TPU:11, one launch (start us, length us, event | category | flops | bytes accessed | tf_op | source)
XLA Modules:
  0.0 111.4 jit_solution(13482725028497448516)
XLA Ops:
  0.6 1.3 %reduce_min.9 = s32[]{:T(128)} reduce(s32[4,6]{1,0:T(4,128)} %param.11, s32[]{:T(128)} %constant.5.clone.1), dimensions={0,1}, to_apply=%region_1.0 | reduce | flops 23 | bytes 104 | tf_op jit(solution)/shard_map/reduce_min | solution.py:321
  2.6 0.7 compare_and_fusion
  3.3 0.8 eq.49.links_ref
  4.0 0.0 copy-start
  4.0 1.2 %broadcast_subtract_fusion.cols_ref = s32[24]{0:T(128)} fusion(s32[24]{0:T(128)S(1)} %eq.49.links_ref, s32[]{:T(128)} %reduce_min.9), kind=kLoop, calls=%fused_computation.15 | loop fusion | flops 24 | bytes 196 | tf_op jit(solution)/shard_map/sub | solution.py:330
  5.2 1.4 %select_reduce_fusion.1.rows_ref = s32[24]{0:T(128)} fusion(s32[128]{0:T(128)} %param.13, s32[24]{0:T(128)S(1)} %eq.49.links_ref), kind=kLoop, calls=%fused_computation.9 | loop fusion | flops 9192 | bytes 704 | tf_op jit(solution)/shard_map/reduce_sum | solution.py:327
  6.6 0.9 convert_reduce_fusion
  7.5 0.7 subtract_add_fusion
  8.2 0.8 select_reduce_fusion
  9.0 1.3 %pad_maximum_fusion.meta_ref = f32[24,128]{1,0:T(8,128)} fusion(f32[8,128]{1,0:T(8,128)S(1)} %broadcast_in_dim.56, f32[16,128]{1,0:T(8,128)} %bitcast.9), kind=kLoop, calls=%fused_computation.8 | loop fusion | flops 3072 | bytes 24576 | tf_op jit(solution)/shard_map/concatenate | solution.py:332
  10.3 17.4 %shard_map.86 = bf16[1024,1024]{1,0:T(8,128)(2,1)} custom-call(s32[24]{0:T(128)} %select_reduce_fusion.1.rows_ref, s32[24]{0:T(128)} %broadcast_subtract_fusion.cols_ref, s32[4]{0:T(128)} %counts_ref.3, bf16[4,1024,1024]{2,1,0:T(8,128)(2,1)} %kinv_ref.3, bf16[4,1024,768]{2,1,0:T(8,128)(2,1)} %coup_ref.3), custom_call_target="tpu_custom_call" | custom-call | tf_op jit(solution)/shard_map/pallas_call | solution.py:56
  27.7 0.0 copy-done
  27.7 68.5 %shard_map.87 = (bf16[4,8,128,1024]{3,2,1,0:T(8,128)(2,1)}, f32[4,8,24,128]{3,2,1,0:T(8,128)}) custom-call(bf16[8,128,1024]{2,1,0:T(8,128)(2,1)} %bitcast.6, f32[24,128]{1,0:T(8,128)} %pad_maximum_fusion.meta_ref), custom_call_target="tpu_custom_call" | custom-call | tf_op jit(solution)/shard_map/pallas_call | solution.py:208
  96.2 1.0 fusion.2
  97.3 1.5 %slice.7 = f32[1,8,16,128]{3,2,1,0:T(8,128)} slice(f32[4,8,24,128]{3,2,1,0:T(8,128)} %get-tuple-element.6), slice={[0:1], [0:8], [0:16], [0:128]} | slice | bytes 131072 | tf_op jit(solution)/shard_map/slice | solution.py:342
  98.7 0.6 convert_element_type.18.codes_ref
  99.3 12.1 %shard_map.88 = (f32[512,1920]{1,0:T(8,128)}, f32[4,1024]{1,0:T(4,128)}) custom-call(s32[32]{0:T(128)} %convert_element_type.18.codes_ref, s32[24]{0:T(128)} %copy-done, s32[4]{0:T(128)} %counts_ref.3, s32[1]{0:T(128)} %bitcast.2.base_ref, bf16[4,1024,1024]{2,1,0:T(8,128)(2,1)} %kinv_ref.3, bf16[4,1024,768]{2,1,0:T(8,128)(2,1)} %coup_ref.3, ...), custom_call_target="tpu_custom_call" | custom-call | tf_op jit(solution)/shard_map/pallas_call | solution.py:284
  (4 shorter events, 0.0 us)
Async XLA Ops:
  4.0 23.7 %copy-start = (s32[24]{0:T(128)}, s32[24]{0:T(128)S(1)}, u32[]{:S(2)}) copy-start(s32[24]{0:T(128)S(1)} %eq.49.links_ref) | copy-start | bytes 292

commit v2 on v1

--- a/solution.py
+++ b/solution.py
@@ -19,55 +19,78 @@
 NT = (((1,), (1,)), ((), ()))
 
 
-def window_kernel(rows_ref, cols_ref, counts_ref, kinv_ref, coup_ref, out_ref, win):
+def window_kernel(
+    links_ref, counts_ref, map_ref, map_row_ref, kinv_ref, coup_ref, out_ref, codes_ref, win
+):
     s = pl.program_id(0)
+    scens = pl.num_programs(0)
+    start = lax.fori_loop(
+        0, scens * K, lambda n, low: jnp.minimum(low, links_ref[n // K, n % K]), NB - 1
+    )
 
     @pl.when(s == 0)
     def _():
         win[...] = jnp.zeros_like(win)
+        lane = lax.broadcasted_iota(jnp.int32, (1, BS), 1)
+        map_row = map_row_ref[...]
+        codes = jnp.full((1, BS), -1, jnp.int32)
+        for w in range(W):
+            block = start + w
+            owner = map_ref[jnp.minimum(block, NB - 1)]
+            earlier = (map_row == owner) & (lane < block)
+            rank = jnp.sum(jnp.where(earlier, 1.0, 0.0), axis=1, keepdims=True).astype(jnp.int32)
+            codes = jnp.where((lane == owner) & (block < NB), rank * W + w, codes)
+        codes_ref[...] = codes
 
     count = counts_ref[s]
     slot = lax.broadcasted_iota(jnp.int32, (R, K * BS), 1) // BS
     coupled = jnp.where(slot < count, coup_ref[0], jnp.zeros((), jnp.bfloat16))
     solved = jnp.dot(kinv_ref[0], coupled, preferred_element_type=jnp.float32)
     solved = solved.astype(jnp.bfloat16)
-    for i in range(K):
+    for i in range(0, K, 2):
 
         @pl.when(i < count)
         def _():
             strip = lax.dot_general(
-                coup_ref[0, :, i * BS : (i + 1) * BS],
-                solved,
-                TN,
-                preferred_element_type=jnp.float32,
+                coupled[:, i * BS : (i + 2) * BS], solved, TN, preferred_element_type=jnp.float32
             )
-            row = pl.multiple_of(rows_ref[s * K + i] * BS, BS)
-            for j in range(K):
-                col = pl.multiple_of(cols_ref[s * K + j] * BS, BS)
-                win[pl.ds(row, BS), pl.ds(col, BS)] += strip[:, j * BS : (j + 1) * BS]
-
-    @pl.when(s == pl.num_programs(0) - 1)
+            for n in range(2):
+                row = pl.multiple_of(map_ref[links_ref[s, i + n]] * BS, BS)
+                for j in range(K):
+                    col = pl.multiple_of((links_ref[s, j] - start) * BS, BS)
+                    win[pl.ds(row, BS), pl.ds(col, BS)] += strip[
+                        n * BS : (n + 1) * BS, j * BS : (j + 1) * BS
+                    ]
+
+    @pl.when(s == scens - 1)
     def _():
         out_ref[...] = win[...].astype(jnp.bfloat16)
 
 
-def windows(rows, cols, counts, kinv, coupling, owners):
+def windows(links, counts, owner_map, kinv, coupling, owners):
     scen_count = kinv.shape[0]
     return pl.pallas_call(
         window_kernel,
-        out_shape=jax.ShapeDtypeStruct((owners * BS, WIN), jnp.bfloat16),
+        out_shape=(
+            jax.ShapeDtypeStruct((owners * BS, WIN), jnp.bfloat16),
+            jax.ShapeDtypeStruct((1, BS), jnp.int32),
+        ),
         grid_spec=pltpu.PrefetchScalarGridSpec(
             num_scalar_prefetch=3,
             grid=(scen_count,),
             in_specs=[
+                pl.BlockSpec((1, NB), lambda s, *_: (0, 0)),
                 pl.BlockSpec((1, R, R), lambda s, *_: (s, 0, 0)),
                 pl.BlockSpec((1, R, K * BS), lambda s, *_: (s, 0, 0)),
             ],
-            out_specs=pl.BlockSpec((owners * BS, WIN), lambda s, *_: (0, 0)),
+            out_specs=(
+                pl.BlockSpec((owners * BS, WIN), lambda s, *_: (0, 0)),
+                pl.BlockSpec((1, BS), lambda s, *_: (0, 0)),
+            ),
             scratch_shapes=[pltpu.VMEM((owners * BS, WIN), jnp.float32)],
         ),
         compiler_params=pltpu.CompilerParams(vmem_limit_bytes=56 * 2**20),
-    )(rows, cols, counts, kinv, coupling)
+    )(links, counts, owner_map, owner_map.reshape(1, NB), kinv, coupling)
 
 
 def flip(index, bits, size):
@@ -83,9 +106,9 @@
 
 
 def exchange_kernel(
-    groups, owners, rows_ref, meta_ref, all_rows, all_meta,
+    groups, owners, rows_ref, first_ref, codes_ref, all_rows, all_table, all_codes,
     own_send, own_recv, x_send, x_recv, core_send, core_recv,
-    meta_send, meta_recv, meta2_send, meta2_recv, local_sem,
+    table_send, table_recv, meta_send, meta_recv, meta2_send, meta2_recv, local_sem,
 ):
     g = lax.axis_index("scen")
     o = lax.axis_index("own")
@@ -118,14 +141,21 @@
     meta = [None] * owners
     for k in range(1, owners):
         meta[k] = remote(
-            meta_ref, all_meta.at[g, o], meta_send.at[k], meta_recv.at[k], (g, partner[k])
-        )
+            codes_ref, all_codes.at[g, o], meta_send.at[k], meta_recv.at[k], (g, partner[k])
+        )
+    table = [None] * owners
+    for k in range(1, owners):
+        table[k] = remote(
+            first_ref, all_table.at[o], table_send.at[k], table_recv.at[k], (g, partner[k])
+        )
+    keep_table = pltpu.make_async_copy(first_ref, all_table.at[o], local_sem.at[2])
     keep_rows = pltpu.make_async_copy(rows_ref.at[o], all_rows.at[g, o], local_sem.at[0])
-    keep_meta = pltpu.make_async_copy(meta_ref, all_meta.at[g, o], local_sem.at[1])
+    keep_meta = pltpu.make_async_copy(codes_ref, all_codes.at[g, o], local_sem.at[1])
 
     far = list(range(owners // 2, owners))
     near = list(range(1, owners // 2))
     keep_meta.start()
+    keep_table.start()
     for k in range(1, owners):
         meta[k].start()
     own[far[0]].start()
@@ -161,13 +191,15 @@
             core_copies[b, k].start()
 
     forward(0)
+    for k in range(1, owners):
+        table[k].start()
     meta2 = []
     keep_meta.wait()
     for k in range(1, owners):
         meta[k].wait()
     for b, other in enumerate(others):
         copy = remote(
-            all_meta.at[g], all_meta.at[g], meta2_send.at[b], meta2_recv.at[b], (other, o)
+            all_codes.at[g], all_codes.at[g], meta2_send.at[b], meta2_recv.at[b], (other, o)
         )
         copy.start()
         meta2.append(copy)
@@ -193,6 +225,9 @@
     for copy in meta2:
         copy.wait()
     keep_rows.wait()
+    keep_table.wait()
+    for k in range(1, owners):
+        table[k].wait()
     for k in near + far[-2:]:
         own[k].wait_send()
     for k in range(owners):
@@ -202,35 +237,42 @@
             core_copies[b, k].wait()
 
 
-def exchange(rows, meta, groups, owners):
+def exchange(rows, first_rows, codes, groups, owners):
     any_space = pl.BlockSpec(memory_space=pl.ANY)
     dma = pltpu.SemaphoreType.DMA
     return pl.pallas_call(
         functools.partial(exchange_kernel, groups, owners),
         out_shape=(
             jax.ShapeDtypeStruct((groups, owners, BS, WIN), jnp.bfloat16),
-            jax.ShapeDtypeStruct((groups, owners) + meta.shape, jnp.float32),
-        ),
-        in_specs=[any_space, any_space],
-        out_specs=(any_space, any_space),
+            jax.ShapeDtypeStruct((owners,) + first_rows.shape, jnp.float32),
+            jax.ShapeDtypeStruct((groups, owners) + codes.shape, jnp.int32),
+        ),
+        in_specs=[any_space] * 3,
+        out_specs=(any_space,) * 3,
         scratch_shapes=[
             dma((owners,)), dma((owners,)),
             dma((groups // 2, owners)), dma((groups // 2, owners)),
             dma((groups // 2, owners)), dma((groups // 2, owners)),
             dma((owners,)), dma((owners,)),
+            dma((owners,)), dma((owners,)),
             dma((groups,)), dma((groups,)),
-            dma((2,)),
+            dma((3,)),
         ],
         compiler_params=pltpu.CompilerParams(collective_id=0, has_side_effects=True),
-    )(rows, meta)
+    )(rows, first_rows, codes)
 
 
 def place_kernel(
-    blocks, sources, codes_ref, links_ref, counts_ref, base_ref,
+    blocks, groups, owners, links_ref, counts_ref, codes_ref,
     kinv_ref, coup_ref, residual_ref, table_ref, rows_ref, band_ref, step_ref, held, sems,
 ):
     s = pl.program_id(0)
-    base = base_ref[0]
+    sources = groups * owners
+    base = lax.axis_index("scen") * blocks
+    me = lax.axis_index("own")
+
+    def code_of(n):
+        return codes_ref[n // owners, n % owners, 0, me]
 
     def copy_of(n):
         return pltpu.make_async_copy(rows_ref.at[n], held.at[n], sems.at[n])
@@ -238,9 +280,10 @@
     @pl.when(s == 0)
     def _():
         def begin(n, carry):
-            rank = codes_ref[n] // W - base
-
-            @pl.when((codes_ref[n] >= 0) & (rank >= 0) & (rank < blocks))
+            code = code_of(n)
+            rank = code // W - base
+
+            @pl.when((code >= 0) & (rank >= 0) & (rank < blocks))
             def _():
                 copy_of(n).start()
 
@@ -251,7 +294,7 @@
     count = counts_ref[s]
     parts = []
     for k in range(K):
-        row = table_ref[pl.ds(links_ref[s * K + k], 1), :]
+        row = table_ref[pl.ds(links_ref[s, k], 1), :]
         parts.append(jnp.where(k < count, row, 0.0))
     picked = jnp.broadcast_to(jnp.concatenate(parts, axis=1), (16, K * BS)).astype(jnp.bfloat16)
     product = lax.dot_general(picked, coup_ref[0], NT, preferred_element_type=jnp.float32)
@@ -264,7 +307,7 @@
         band_ref[...] = jnp.zeros_like(band_ref)
 
         def add(n, carry):
-            code = codes_ref[n]
+            code = code_of(n)
 
             @pl.when((code >= 0) & (code // W - base == s))
             def _():
@@ -277,20 +320,22 @@
         lax.fori_loop(0, sources, add, 0)
 
 
-def place(codes, links, counts, base, kinv, coupling, residual, table, rows, blocks):
+def place(links, counts, codes, kinv, coupling, residual, table, rows, blocks):
     scen_count = kinv.shape[0]
-    sources = rows.shape[0]
+    groups, owners = codes.shape[:2]
+    sources = groups * owners
     assert blocks <= scen_count
     return pl.pallas_call(
-        functools.partial(place_kernel, blocks, sources),
+        functools.partial(place_kernel, blocks, groups, owners),
         out_shape=(
             jax.ShapeDtypeStruct((blocks * BS, BAND), jnp.float32),
             jax.ShapeDtypeStruct((scen_count, R), jnp.float32),
         ),
         grid_spec=pltpu.PrefetchScalarGridSpec(
-            num_scalar_prefetch=4,
+            num_scalar_prefetch=2,
             grid=(scen_count,),
             in_specs=[
+                pl.BlockSpec(memory_space=pltpu.SMEM),
                 pl.BlockSpec((1, R, R), lambda s, *_: (s, 0, 0)),
                 pl.BlockSpec((1, R, K * BS), lambda s, *_: (s, 0, 0)),
                 pl.BlockSpec((scen_count, R), lambda s, *_: (0, 0)),
@@ -307,44 +352,19 @@
             ],
         ),
         compiler_params=pltpu.CompilerParams(vmem_limit_bytes=58 * 2**20),
-    )(codes, links, counts, base, kinv, coupling, residual, table, rows)
+    )(links, counts, codes, kinv, coupling, residual, table, rows)
 
 
 def local(kinv, coupling, residual, first_step, links, counts, owner_map):
     groups = lax.axis_size("scen")
     owners = lax.axis_size("own")
-    row_blocks = NB // owners
-    blocks = row_blocks // groups
-    positions = jnp.arange(NB, dtype=jnp.int32)
-    same_owner = owner_map[:, None] == owner_map[None, :]
-    rank = jnp.sum(same_owner & (positions[None, :] < positions[:, None]), axis=1, dtype=jnp.int32)
-    start = jnp.min(links)
-    inside = (positions >= start) & (positions < start + W)
-    lanes = jnp.arange(BS, dtype=jnp.int32)
-    holds = inside[:, None] & (owner_map[:, None] == lanes[None, :])
-    codes = jnp.sum(jnp.where(holds, (rank * W + positions - start + 1)[:, None], 0), axis=0) - 1
-    flat_links = links.reshape(-1)
-    owner_of = jnp.sum(
-        jnp.where(flat_links[:, None] == positions[None, :], owner_map[None, :], 0), axis=1
-    )
-    rows = windows(owner_of, flat_links - start, counts, kinv, coupling, owners)
-    table_rows = first_step.shape[0] // BS
-    meta = jnp.concatenate(
-        [
-            first_step.reshape(table_rows, BS),
-            jnp.broadcast_to(codes.astype(jnp.float32)[None], (8, BS)),
-        ],
-        axis=0,
-    )
-    all_rows, all_meta = exchange(rows.reshape(owners, BS, WIN), meta, groups, owners)
-    g = lax.axis_index("scen")
-    o = lax.axis_index("own")
-    table = all_meta[0, :, :table_rows].reshape(NB, BS)
-    mine = jnp.sum(
-        jnp.where(lanes == o, all_meta[:, :, table_rows].reshape(groups * owners, BS), 0.0), axis=1
-    ).astype(jnp.int32)
+    blocks = NB // owners // groups
+    rows, codes = windows(links, counts, owner_map, kinv, coupling, owners)
+    all_rows, all_table, all_codes = exchange(
+        rows.reshape(owners, BS, WIN), first_step.reshape(-1, BS), codes, groups, owners
+    )
     band, second_step = place(
-        mine, flat_links, counts, (g * blocks).reshape(1), kinv, coupling, residual, table,
+        links, counts, all_codes, kinv, coupling, residual, all_table.reshape(NB, BS),
         all_rows.reshape(groups * owners, BS, WIN), blocks,
     )
     return band[None], second_step

time: 111 us -> 97.3 us (0.88)
  other arithmetic: 9.26 us -> 0 us
  local copies, waits for them, and re-layouts: 2.8 us -> 0 us
  Pallas kernels: 98 us -> 96.2 us
    pallas_call x1, Pallas kernels: 68.5 us -> 62.8 us  [exchange(): pl.pallas_call(functools.partial(exchange_kernel, groups, owners), out_sh...]
    reduce_sum x4 -> x0, other arithmetic: 4.16 us -> none  [the longest x1 1.43 us: local(): jnp.sum(jnp.where(flat_links[:, None] == positions[None, :], owner_map[No...]
    pallas_call x2, Pallas kernels: 29.5 us -> 33.4 us  [the longest x1 20.1 us: windows(): pl.pallas_call(window_kernel, out_shape=(jax.ShapeDtypeStruct((owners * B...]
    slice x1 -> x0, local copies, waits for them, and re-layouts: 1.46 us -> none  [local(): table = all_meta[0, :, :table_rows].reshape(NB, BS)]
    reduce_min x1 -> x0, other arithmetic: 1.32 us -> none  [local(): start = jnp.min(links)]
    concatenate x1 -> x0, other arithmetic: 1.3 us -> none  [local(): jnp.concatenate([first_step.reshape(table_rows, BS), jnp.broadcast_to(cod...]
    sub x1 -> x0, other arithmetic: 1.15 us -> none  [local(): rows = windows(owner_of, flat_links - start, counts, kinv, coupling, owners)]
where the time goes in v2:
time: 97.3 us; the launch traced here: 96.8 us
  Pallas kernels  96.2 us (99%)
    pallas_call x1, Pallas kernels, exchange(): pl.pallas_call(functools.partial(exchange_kernel, groups, owners), out_sh...  62.8 us
    pallas_call x1, Pallas kernels, windows(): pl.pallas_call(window_kernel, out_shape=(jax.ShapeDtypeStruct((owners * B...  20.1 us
    pallas_call x1, Pallas kernels, place(): pl.pallas_call(functools.partial(place_kernel, blocks, groups, owners), o...  13.3 us

profile of v2, /device:TPU:11, one launch (start us, length us, event | category | flops | bytes accessed | tf_op | source)
XLA Modules:
  0.0 96.8 jit_solution(863856495758028600)
XLA Ops:
  0.6 20.1 %shard_map.86 = (bf16[1024,1024]{1,0:T(8,128)(2,1)}, s32[1,128]{1,0:T(1,128)}) custom-call(s32[4,6]{1,0:T(4,128)} %links_ref.3, s32[4]{0:T(128)} %counts_ref.3, s32[128]{0:T(128)} %map_ref.1, s32[1,128]{1,0:T(1,128)} %bitcast.10, bf16[4,1024,1024]{2,1,0:T(8,128)(2,1)} %kinv_ref.3, bf16[4,1024,768]{2,1,0:T(8,128)(2,1)} %coup_ref.3), custom_call_target="tpu_custom_call" | custom-call | tf_op jit(solution)/shard_map/pallas_call | solution.py:72
  20.7 62.8 %shard_map.87 = (bf16[4,8,128,1024]{3,2,1,0:T(8,128)(2,1)}, f32[8,16,128]{2,1,0:T(8,128)}, s32[4,8,1,128]{3,2,1,0:T(1,128)}) custom-call(bf16[8,128,1024]{2,1,0:T(8,128)(2,1)} %bitcast.7, f32[16,128]{1,0:T(8,128)} %bitcast.9, s32[1,128]{1,0:T(1,128)} %get-tuple-element.10.codes_ref), custom_call_target="tpu_custom_call" | custom-call | tf_op jit(solution)/shard_map/pallas_call | solution.py:243
  83.5 13.3 %shard_map.88 = (f32[512,1920]{1,0:T(8,128)}, f32[4,1024]{1,0:T(4,128)}) custom-call(s32[4,6]{1,0:T(4,128)} %links_ref.3, s32[4]{0:T(128)} %counts_ref.3, s32[4,8,1,128]{3,2,1,0:T(1,128)} %get-tuple-element.11.codes_ref, bf16[4,1024,1024]{2,1,0:T(8,128)(2,1)} %kinv_ref.3, bf16[4,1024,768]{2,1,0:T(8,128)(2,1)} %coup_ref.3, f32[4,1024]{1,0:T(4,128)} %residual_ref.1, ...), custom_call_target="tpu_custom_call" | custom-call | tf_op jit(solution)/shard_map/pallas_call | solution.py:328
